TPU v7x, 32 devices: a whole 2x2x4 slice. The times are simulated.
32 devices in a mesh: seq: 8 (over z, x), head: 4 (over y, core).
Axes of the slice: x: 2, y: 2, z: 4, core: 2. Of those that a mesh axis runs over, the one named last changes fastest.
Arguments:
- queries: bfloat16 [2048, 2048], P('seq', 'head'), may hold values from -30 to 30, as said below
- keys: bfloat16 [2048, 2048], P('seq', 'head'), may hold values from -30 to 30, as said below
- values: bfloat16 [2048, 2048], P('seq', 'head'), may hold values from -6 to 6
- out_grad: bfloat16 [2048, 2048], P('seq', 'head'), may hold values from -6 to 6
- rand_blocks: int32 [16, 16, 3], P('head', 'seq'), may hold values from 0 to 15, as said below
Outputs:
- attn_out: bfloat16 [2048, 2048], P('seq', 'head')
- grad_queries: bfloat16 [2048, 2048], P('seq', 'head')
- grad_keys: bfloat16 [2048, 2048], P('seq', 'head')
- grad_values: bfloat16 [2048, 2048], P('seq', 'head')
Inputs may be any that keep to these rules, and one draw needn't show every extreme that they name: queries are of order one; in some draws a few rows reach larger scales. keys are of order one; in some draws a few rows reach larger scales. `rand_blocks`: for each aligned group of 4 heads and each aligned run of 2 query blocks, at most 3 of the group's entries name blocks of one aligned run of 2 key blocks, and in every group some run is named exactly 3 times.
All inputs are finite; a program needn't handle non-finite values.
Results may differ from a plain program's by a relative error of at most 0.015.
The roundings to bfloat16 on the way count: a program that leaves them out, or rounds other values in their place, can miss the bound.
Values may be sent and summed in bfloat16 or wider, within the bound.
A program may use at most 192 MiB of HBM per device.

v0:
```python
import math

import jax
import jax.numpy as jnp
from jax import lax
from jax.sharding import PartitionSpec as P


def swapped(value, axis, distance):
    mask = 2**distance
    pairs = [(source, source ^ mask) for source in range(lax.axis_size(axis))]
    return lax.ppermute(value, axis, pairs)


def round_trip(value_arr):
    return lax.optimization_barrier(value_arr.astype(jnp.bfloat16)).astype(jnp.float32)


def near_partner(block_arr, near_bit):
    span_size = 1 << near_bit
    folded = block_arr.reshape(
        (block_arr.shape[0] // (2 * span_size), 2, span_size) + block_arr.shape[1:]
    )
    return folded[:, ::-1].reshape(block_arr.shape)


def slot_terms(grad_scores, weights_low, query_rows, grad_rows, first_slot, last_slot, score_scale):
    key_terms = score_scale * jnp.einsum(
        "btks,btd->bksd",
        grad_scores[:, :, first_slot:last_slot],
        query_rows,
        preferred_element_type=jnp.float32,
    )
    value_terms = jnp.einsum(
        "btks,btd->bksd",
        weights_low[:, :, first_slot:last_slot],
        grad_rows,
        preferred_element_type=jnp.float32,
    )
    return (key_terms, value_terms)


def listed_rows(own_four, near_list, far_list, rand_part, head_index):
    part_list = [own_four[:, :, head_index]]
    part_list = part_list + [near_arr[:, :, head_index] for near_arr in near_list]
    part_list = part_list + [far_arr[:, :, head_index] for far_arr in far_list]
    return jnp.concatenate([jnp.stack(part_list, axis=1), rand_part[head_index]], axis=1)


def local(queries, keys, values, out_grad, rand_blocks):
    tok_rows = queries.shape[0]
    heads_here, blk_count, rand_count = rand_blocks.shape
    head_size = queries.shape[1] // heads_here
    blk_size = tok_rows // blk_count
    score_scale = 1.0 / math.sqrt(head_size)
    seq_devices = lax.axis_size("seq")
    far_count = seq_devices.bit_length() - 1
    near_count = blk_count.bit_length() - 1
    block_shape = (blk_count, blk_size, heads_here, head_size)
    query_four = queries.reshape(block_shape)
    key_four = keys.reshape(block_shape)
    value_four = values.reshape(block_shape)
    grad_four = out_grad.reshape(block_shape)
    far_keys = []
    far_values = []
    for far_level in range(far_count):
        got_keys, got_values = swapped((keys, values), "seq", far_level)
        far_keys.append(got_keys.reshape(block_shape))
        far_values.append(got_values.reshape(block_shape))
    near_keys = [near_partner(key_four, 0)]
    near_values = [near_partner(value_four, 0)]
    total_req = heads_here * blk_count * rand_count
    slot_cap = max(2, -(-total_req // seq_devices))
    slot_count = seq_devices * slot_cap
    flat_req = rand_blocks.reshape(-1)
    owner_dev = flat_req // blk_count
    req_index = jnp.arange(total_req, dtype=jnp.int32)
    req_head = req_index // (blk_count * rand_count)
    payload = req_head * blk_count + flat_req % blk_count
    earlier_same = (owner_dev[:, None] == owner_dev[None, :]) & (
        req_index[:, None] > req_index[None, :]
    )
    slot_rank = jnp.sum(earlier_same.astype(jnp.int32), axis=1)
    slot_of_req = owner_dev * slot_cap + slot_rank
    slot_match = slot_of_req[None, :] == jnp.arange(slot_count, dtype=jnp.int32)[:, None]
    filled = jnp.any(slot_match, axis=1)
    req_of_slot = jnp.sum(jnp.where(slot_match, req_index[None, :], 0), axis=1)
    send_ids = jnp.where(filled, jnp.sum(jnp.where(slot_match, payload[None, :], 0), axis=1), -1)
    send_ids = send_ids.reshape(seq_devices, slot_cap)
    asked_ids = lax.all_to_all(send_ids, "seq", split_axis=0, concat_axis=0, tiled=True)
    out_shape = asked_ids.shape + (blk_size, head_size)
    safe_ids = jnp.maximum(asked_ids.reshape(-1), 0)
    pick_head = safe_ids // blk_count
    pick_blk = safe_ids % blk_count
    key_pick = key_four[pick_blk, :, pick_head, :]
    value_pick = value_four[pick_blk, :, pick_head, :]
    key_back = lax.all_to_all(
        key_pick.reshape(out_shape), "seq", split_axis=0, concat_axis=0, tiled=True
    )
    value_back = lax.all_to_all(
        value_pick.reshape(out_shape), "seq", split_axis=0, concat_axis=0, tiled=True
    )
    key_slots, value_slots, asked_ids = (key_back, value_back, asked_ids)
    rand_shape = (heads_here, blk_count, rand_count, blk_size, head_size)
    rand_keys = key_slots.reshape(slot_count, blk_size, head_size)[slot_of_req].reshape(rand_shape)
    rand_values = value_slots.reshape(slot_count, blk_size, head_size)[slot_of_req].reshape(
        rand_shape
    )
    asked_flat = asked_ids.reshape(-1)
    key_sets = []
    value_sets = []
    weight_keep = []
    weight_low_keep = []
    attn_heads = []
    total_heads = []
    for head_index in range(heads_here):
        key_set = listed_rows(key_four, near_keys, far_keys, rand_keys, head_index)
        value_set = listed_rows(value_four, near_values, far_values, rand_values, head_index)
        scores = (
            jnp.einsum(
                "btd,bksd->btks",
                query_four[:, :, head_index],
                key_set,
                preferred_element_type=jnp.float32,
            )
            * score_scale
        )
        row_max = jnp.max(scores, axis=(2, 3))
        log_total = row_max + jnp.log(
            jnp.sum(jnp.exp(scores - row_max[:, :, None, None]), axis=(2, 3))
        )
        weights = jnp.exp(scores - log_total[:, :, None, None])
        weights_low = weights.astype(jnp.bfloat16)
        attn_heads.append(
            jnp.einsum(
                "btks,bksd->btd", weights_low, value_set, preferred_element_type=jnp.float32
            ).astype(jnp.bfloat16)
        )
        total_heads.append(log_total)
        key_sets.append(key_set)
        value_sets.append(value_set)
        weight_keep.append(weights)
        weight_low_keep.append(weights_low)
    attn_four = jnp.stack(attn_heads, axis=2)
    row_deltas = jnp.sum(grad_four.astype(jnp.float32) * attn_four.astype(jnp.float32), axis=3)
    slot_shape = (seq_devices, slot_cap, blk_size, head_size)
    far_first = 1 + near_count
    rand_first = far_first + far_count
    query_heads = []
    key_heads = []
    value_heads = []
    far_key_parts = []
    far_value_parts = []
    rand_key_parts = []
    rand_value_parts = []
    for head_index in range(heads_here):
        query_rows = query_four[:, :, head_index]
        grad_rows = grad_four[:, :, head_index]
        grad_weights = jnp.einsum(
            "btd,bksd->btks", grad_rows, value_sets[head_index], preferred_element_type=jnp.float32
        )
        grad_scores = (
            weight_keep[head_index]
            * (grad_weights - row_deltas[:, :, head_index][:, :, None, None])
        ).astype(jnp.bfloat16)
        query_heads.append(
            (
                score_scale
                * jnp.einsum(
                    "btks,bksd->btd",
                    grad_scores,
                    key_sets[head_index],
                    preferred_element_type=jnp.float32,
                )
            ).astype(jnp.bfloat16)
        )
        weights_low = weight_low_keep[head_index]
        own_keys, own_values = slot_terms(
            grad_scores, weights_low, query_rows, grad_rows, 0, far_first, score_scale
        )
        key_acc = own_keys[:, 0]
        value_acc = own_values[:, 0]
        key_acc = key_acc + near_partner(round_trip(own_keys[:, 1]), 0)
        value_acc = value_acc + near_partner(round_trip(own_values[:, 1]), 0)
        far_keys_part, far_values_part = slot_terms(
            grad_scores, weights_low, query_rows, grad_rows, far_first, rand_first, score_scale
        )
        far_key_parts.append(far_keys_part.astype(jnp.bfloat16))
        far_value_parts.append(far_values_part.astype(jnp.bfloat16))
        rand_keys_part, rand_values_part = slot_terms(
            grad_scores,
            weights_low,
            query_rows,
            grad_rows,
            rand_first,
            rand_first + rand_count,
            score_scale,
        )
        rand_key_parts.append(rand_keys_part.astype(jnp.bfloat16))
        rand_value_parts.append(rand_values_part.astype(jnp.bfloat16))
        key_heads.append(key_acc)
        value_heads.append(value_acc)
    key_grad = jnp.stack(key_heads, axis=2)
    value_grad = jnp.stack(value_heads, axis=2)
    far_key_all = jnp.stack(far_key_parts, axis=3)
    far_value_all = jnp.stack(far_value_parts, axis=3)
    for far_level in range(far_count):
        send_keys = far_key_all[:, far_level].reshape(tok_rows, heads_here * head_size)
        send_values = far_value_all[:, far_level].reshape(tok_rows, heads_here * head_size)
        back_keys, back_values = swapped((send_keys, send_values), "seq", far_level)
        key_grad = key_grad + back_keys.reshape(block_shape).astype(jnp.float32)
        value_grad = value_grad + back_values.reshape(block_shape).astype(jnp.float32)
    rand_key_all = jnp.stack(rand_key_parts, axis=0).reshape(total_req, blk_size, head_size)
    rand_value_all = jnp.stack(rand_value_parts, axis=0).reshape(total_req, blk_size, head_size)
    empty_slot = jnp.zeros((slot_count, blk_size, head_size), jnp.bfloat16)
    send_keys = jnp.where(filled[:, None, None], rand_key_all[req_of_slot], empty_slot).reshape(
        slot_shape
    )
    send_values = jnp.where(filled[:, None, None], rand_value_all[req_of_slot], empty_slot).reshape(
        slot_shape
    )
    slot_keys, slot_values = (
        lax.all_to_all(send_keys, "seq", split_axis=0, concat_axis=0, tiled=True),
        lax.all_to_all(send_values, "seq", split_axis=0, concat_axis=0, tiled=True),
    )
    target_rows = jnp.arange(heads_here * blk_count, dtype=jnp.int32)
    onehot = (asked_flat[None, :] == target_rows[:, None]).astype(jnp.bfloat16)
    extra_keys = jnp.dot(
        onehot,
        slot_keys.reshape(slot_count, blk_size * head_size),
        preferred_element_type=jnp.float32,
    )
    extra_values = jnp.dot(
        onehot,
        slot_values.reshape(slot_count, blk_size * head_size),
        preferred_element_type=jnp.float32,
    )
    extra_keys = extra_keys.reshape(heads_here, blk_count, blk_size, head_size).transpose(
        1, 2, 0, 3
    )
    extra_values = extra_values.reshape(heads_here, blk_count, blk_size, head_size).transpose(
        1, 2, 0, 3
    )
    attn_out = attn_four.reshape(tok_rows, heads_here * head_size)
    grad_queries = jnp.stack(query_heads, axis=2).reshape(tok_rows, heads_here * head_size)
    grad_keys = (
        (key_grad + extra_keys).astype(jnp.bfloat16).reshape(tok_rows, heads_here * head_size)
    )
    grad_values = (
        (value_grad + extra_values).astype(jnp.bfloat16).reshape(tok_rows, heads_here * head_size)
    )
    return (attn_out, grad_queries, grad_keys, grad_values)


def solution(mesh):
    return jax.shard_map(
        local,
        mesh=mesh,
        in_specs=(
            P("seq", "head"),
            P("seq", "head"),
            P("seq", "head"),
            P("seq", "head"),
            P("head", "seq", None),
        ),
        out_specs=(P("seq", "head"), P("seq", "head"), P("seq", "head"), P("seq", "head")),
        check_vma=False,
    )
```

profile of v0, /device:TPU:0, one launch (start us, length us, event | category | flops | bytes accessed | tf_op | source)
XLA Modules:
  0.0 234.3 jit_solution(2141892687122663802)
XLA Ops:
  0.6 3.0 %collective-permute-start = (bf16[256,512]{1,0:T(8,128)(2,1)}, bf16[256,512]{1,0:T(8,128)(2,1)}, u32[]{:S(2)}, u32[]{:S(2)}) collective-permute-start(bf16[256,512]{1,0:T(8,128)(2,1)} %param.6), channel_id=1, source_target_pairs={{0,4},{4,0},{8,12},{12,8},{16,20},{20,16},{24,28},{28,24},{1,5},{5... | collective-permute-start | bytes 786440 | tf_op jit(solution)/shard_map/ppermute | solution.py:12
  3.6 2.6 %collective-permute-start.2 = (bf16[256,512]{1,0:T(8,128)(2,1)}, bf16[256,512]{1,0:T(8,128)(2,1)}, u32[]{:S(2)}, u32[]{:S(2)}) collective-permute-start(bf16[256,512]{1,0:T(8,128)(2,1)} %param.6), channel_id=1, source_target_pairs={{0,16},{4,20},{8,24},{12,28},{16,0},{20,4},{24,8},{28,12},{1,17},{... | collective-permute-start | bytes 786440 | tf_op jit(solution)/shard_map/ppermute | solution.py:12
  6.2 1.6 collective-permute-start.1
  10.7 4.8 %all-to-all-start = ((s32[8,1,3]{2,1,0:T(1,128)}), s32[8,1,3]{2,1,0:T(1,128)S(1)}, u32[]{:S(2)}, u32[]{:S(2)}) async-start(s32[8,1,3]{2,1,0:T(1,128)} %bitcast.6), calls=%async_computation | async-start | bytes 8192 | tf_op jit(solution)/shard_map/all_to_all | solution.py:90
  16.7 1.1 reshape.562
  20.7 1.1 fusion.158
  21.9 1.1 fusion.163
  33.9 1.6 gather_fusion
  35.5 6.0 %all-to-all-start.1 = ((bf16[8,3,128,128]{3,2,1,0:T(8,128)(2,1)}), bf16[8,3,128,128]{3,2,1,0:T(8,128)(2,1)S(1)}, u32[]{:S(2)}, u32[]{:S(2)}) async-start(bf16[8,3,128,128]{3,2,1,0:T(8,128)(2,1)} %bitcast.8), calls=%async_computation.1 | async-start | bytes 1572864 | tf_op jit(solution)/shard_map/all_to_all | solution.py:97
  41.5 1.6 gather_fusion.2
  43.2 2.0 collective-permute-start.4
  46.2 1.2 fusion.162
  48.4 1.2 fusion.160
  50.6 1.2 fusion.166
  52.8 1.2 fusion.164
  53.9 1.7 copy.525
  62.4 1.2 fusion.161
  64.6 1.2 fusion.165
  65.7 1.7 copy.526
  85.1 4.6 %all-to-all-start.2 = ((bf16[8,3,128,128]{3,2,1,0:T(8,128)(2,1)}), bf16[8,3,128,128]{3,2,1,0:T(8,128)(2,1)}, u32[]{:S(2)}, u32[]{:S(2)}) async-start(bf16[8,3,128,128]{3,2,1,0:T(8,128)(2,1)} %bitcast.23), calls=%async_computation.2 | async-start | bytes 1572864 | tf_op jit(solution)/shard_map/all_to_all | solution.py:100
  103.3 3.9 %all-to-all-done.2 = bf16[8,3,128,128]{3,2,1,0:T(8,128)(2,1)} async-done(((bf16[8,3,128,128]{3,2,1,0:T(8,128)(2,1)}), bf16[8,3,128,128]{3,2,1,0:T(8,128)(2,1)}, u32[]{:S(2)}, u32[]{:S(2)}) %all-to-all-start.2) | async-done | bytes 786464 | tf_op jit(solution)/shard_map/all_to_all | solution.py:100
  107.2 2.8 %gather_fusion.3 = bf16[24,128,128]{2,1,0:T(8,128)(2,1)} fusion(bf16[24,128,128]{2,1,0:T(8,128)(2,1)} %bitcast.24, s32[1024]{0:T(1024)} %copy-done.120), kind=kCustom, calls=%fused_computation.3 | custom fusion | bytes 1572960 | tf_op jit(solution)/shard_map/gather | solution.py:106
  110.0 2.1 fusion.157
  112.1 1.8 copy.397
  113.9 1.7 copy.422
  115.6 1.7 copy.409
  117.4 1.7 copy.435
  119.1 1.7 constant_dynamic-update-slice_fusion.12
  120.8 1.6 fusion.54
  148.2 1.3 pad_maximum_fusion.3
  150.8 1.3 broadcast_select_fusion
  152.2 3.5 %all-to-all-start.4 = ((bf16[8,3,128,128]{3,2,1,0:T(8,128)(2,1)}), bf16[8,3,128,128]{3,2,1,0:T(8,128)(2,1)S(1)}, u32[]{:S(2)}, u32[]{:S(2)}) async-start(bf16[8,3,128,128]{3,2,1,0:T(8,128)(2,1)} %get-tuple-element.75), calls=%async_computation.4 | async-start | bytes 1572864 | tf_op jit(solution)/shard_map/all_to_all | solution.py:224
  156.7 2.0 collective-permute-start.7
  158.7 1.5 fusion.105
  164.8 10.2 %all-to-all-done.4 = bf16[8,3,128,128]{3,2,1,0:T(8,128)(2,1)S(1)} async-done(((bf16[8,3,128,128]{3,2,1,0:T(8,128)(2,1)}), bf16[8,3,128,128]{3,2,1,0:T(8,128)(2,1)S(1)}, u32[]{:S(2)}, u32[]{:S(2)}) %all-to-all-start.4) | async-done | bytes 786464 | tf_op jit(solution)/shard_map/all_to_all | solution.py:224
  175.0 3.9 %all-to-all-start.3 = ((bf16[8,3,128,128]{3,2,1,0:T(8,128)(2,1)}), bf16[8,3,128,128]{3,2,1,0:T(8,128)(2,1)S(1)}, u32[]{:S(2)}, u32[]{:S(2)}) async-start(bf16[8,3,128,128]{3,2,1,0:T(8,128)(2,1)} %get-tuple-element.76), calls=%async_computation.3 | async-start | bytes 1572864 | tf_op jit(solution)/shard_map/all_to_all | solution.py:223
  185.7 2.8 %collective-permute-start.8 = (bf16[256,512]{1,0:T(8,128)(2,1)S(1)}, bf16[256,512]{1,0:T(8,128)(2,1)S(1)}, u32[]{:S(2)}, u32[]{:S(2)}) collective-permute-start(bf16[256,512]{1,0:T(8,128)(2,1)S(1)} %bitcast.675), channel_id=1, source_target_pairs={{0,16},{4,20},{8,24},{12,28},{16,0},{20,4},{24,8},{28,12},{1,17},{... | collective-permute-start | bytes 786440 | tf_op jit(solution)/shard_map/ppermute | solution.py:12
  188.5 1.5 collective-permute-start.10
  190.5 1.5 collective-permute-start.9
  196.2 1.1 reshape.589
  197.3 19.9 %collective-permute-done.8 = bf16[256,512]{1,0:T(8,128)(2,1)S(1)} collective-permute-done((bf16[256,512]{1,0:T(8,128)(2,1)S(1)}, bf16[256,512]{1,0:T(8,128)(2,1)S(1)}, u32[]{:S(2)}, u32[]{:S(2)}) %collective-permute-start.8) | collective-permute-done | bytes 262176 | tf_op jit(solution)/shard_map/ppermute | solution.py:12
  217.4 1.1 reshape.592
  218.5 3.1 %collective-permute-done.11 = bf16[256,512]{1,0:T(8,128)(2,1)} collective-permute-done((bf16[256,512]{1,0:T(8,128)(2,1)}, bf16[256,512]{1,0:T(8,128)(2,1)}, u32[]{:S(2)}, u32[]{:S(2)}) %collective-permute-start.11) | collective-permute-done | bytes 262176 | tf_op jit(solution)/shard_map/ppermute | solution.py:12
  221.6 1.9 reshape.593
  223.5 1.9 reshape.591
  225.4 1.9 reshape.588
  228.0 1.5 fusion.64
  230.7 1.3 fusion.75
  (476 shorter events, 108.6 us)
Async XLA Ops:
  0.6 42.5 %collective-permute-start = (bf16[256,512]{1,0:T(8,128)(2,1)}, bf16[256,512]{1,0:T(8,128)(2,1)}, u32[]{:S(2)}, u32[]{:S(2)}) collective-permute-start(bf16[256,512]{1,0:T(8,128)(2,1)} %param.6), channel_id=1, source_target_pairs={{0,4},{4,0},{8,12},{12,8},{16,20},{20,16},{24,28},{28,24},{1,5},{5... | collective-permute-start | bytes 786440 | tf_op jit(solution)/shard_map/ppermute | solution.py:12
  3.6 43.8 %collective-permute-start.2 = (bf16[256,512]{1,0:T(8,128)(2,1)}, bf16[256,512]{1,0:T(8,128)(2,1)}, u32[]{:S(2)}, u32[]{:S(2)}) collective-permute-start(bf16[256,512]{1,0:T(8,128)(2,1)} %param.6), channel_id=1, source_target_pairs={{0,16},{4,20},{8,24},{12,28},{16,0},{20,4},{24,8},{28,12},{1,17},{... | collective-permute-start | bytes 786440 | tf_op jit(solution)/shard_map/ppermute | solution.py:12
  6.2 55.1 %collective-permute-start.1 = (bf16[256,512]{1,0:T(8,128)(2,1)}, bf16[256,512]{1,0:T(8,128)(2,1)}, u32[]{:S(2)}, u32[]{:S(2)}) collective-permute-start(bf16[256,512]{1,0:T(8,128)(2,1)} %param.6), channel_id=1, source_target_pairs={{0,8},{4,12},{8,0},{12,4},{16,24},{20,28},{24,16},{28,20},{1,9},{5... | collective-permute-start | bytes 786440 | tf_op jit(solution)/shard_map/ppermute | solution.py:12
  7.8 41.8 %collective-permute-start.3 = (bf16[256,512]{1,0:T(8,128)(2,1)}, bf16[256,512]{1,0:T(8,128)(2,1)}, u32[]{:S(2)}, u32[]{:S(2)}) collective-permute-start(bf16[256,512]{1,0:T(8,128)(2,1)} %param.7), channel_id=1, source_target_pairs={{0,4},{4,0},{8,12},{12,8},{16,20},{20,16},{24,28},{28,24},{1,5},{5... | collective-permute-start | bytes 786440 | tf_op jit(solution)/shard_map/ppermute | solution.py:12
  8.3 43.4 %collective-permute-start.5 = (bf16[256,512]{1,0:T(8,128)(2,1)}, bf16[256,512]{1,0:T(8,128)(2,1)}, u32[]{:S(2)}, u32[]{:S(2)}) collective-permute-start(bf16[256,512]{1,0:T(8,128)(2,1)} %param.7), channel_id=1, source_target_pairs={{0,16},{4,20},{8,24},{12,28},{16,0},{20,4},{24,8},{28,12},{1,17},{... | collective-permute-start | bytes 786440 | tf_op jit(solution)/shard_map/ppermute | solution.py:12
  10.7 21.1 %all-to-all-start = ((s32[8,1,3]{2,1,0:T(1,128)}), s32[8,1,3]{2,1,0:T(1,128)S(1)}, u32[]{:S(2)}, u32[]{:S(2)}) async-start(s32[8,1,3]{2,1,0:T(1,128)} %bitcast.6), calls=%async_computation | async-start | bytes 8192 | tf_op jit(solution)/shard_map/all_to_all | solution.py:90
  24.0 65.7 %copy-start.120 = (s32[1024]{0:T(1024)}, s32[1024]{0:T(1024)S(1)}, u32[]{:S(2)}) copy-start(s32[1024]{0:T(1024)S(1)} %pad_clamp_fusion.1) | copy-start | bytes 12292
  35.5 49.6 %all-to-all-start.1 = ((bf16[8,3,128,128]{3,2,1,0:T(8,128)(2,1)}), bf16[8,3,128,128]{3,2,1,0:T(8,128)(2,1)S(1)}, u32[]{:S(2)}, u32[]{:S(2)}) async-start(bf16[8,3,128,128]{3,2,1,0:T(8,128)(2,1)} %bitcast.8), calls=%async_computation.1 | async-start | bytes 1572864 | tf_op jit(solution)/shard_map/all_to_all | solution.py:97
  43.2 20.4 %collective-permute-start.4 = (bf16[256,512]{1,0:T(8,128)(2,1)}, bf16[256,512]{1,0:T(8,128)(2,1)}, u32[]{:S(2)}, u32[]{:S(2)}) collective-permute-start(bf16[256,512]{1,0:T(8,128)(2,1)} %param.7), channel_id=1, source_target_pairs={{0,8},{4,12},{8,0},{12,4},{16,24},{20,28},{24,16},{28,20},{1,9},{5... | collective-permute-start | bytes 786440 | tf_op jit(solution)/shard_map/ppermute | solution.py:12
  71.6 5.2 %copy-start.13 = (bf16[2,8,128,128]{2,3,1,0:T(8,128)(2,1)}, bf16[2,8,128,128]{2,3,1,0:T(8,128)(2,1)S(1)}, u32[]{:S(2)}) copy-start(bf16[2,8,128,128]{2,3,1,0:T(8,128)(2,1)S(1)} %constant_dynamic-update-slice_fusion.1) | copy-start | bytes 1572868
  73.3 5.7 %copy-start.9 = (bf16[2,8,128,128]{2,3,1,0:T(8,128)(2,1)}, bf16[2,8,128,128]{2,3,1,0:T(8,128)(2,1)S(1)}, u32[]{:S(2)}) copy-start(bf16[2,8,128,128]{2,3,1,0:T(8,128)(2,1)S(1)} %constant_dynamic-update-slice_fusion.13) | copy-start | bytes 1572868
  75.9 4.6 %copy-start.11 = (bf16[2,8,128,128]{2,3,1,0:T(8,128)(2,1)}, bf16[2,8,128,128]{2,3,1,0:T(8,128)(2,1)S(1)}, u32[]{:S(2)}) copy-start(bf16[2,8,128,128]{2,3,1,0:T(8,128)(2,1)S(1)} %constant_dynamic-update-slice_fusion.25) | copy-start | bytes 1572868
  76.9 5.0 %copy-start.7 = (bf16[2,8,128,128]{2,3,1,0:T(8,128)(2,1)}, bf16[2,8,128,128]{2,3,1,0:T(8,128)(2,1)S(1)}, u32[]{:S(2)}) copy-start(bf16[2,8,128,128]{2,3,1,0:T(8,128)(2,1)S(1)} %constant_dynamic-update-slice_fusion.37) | copy-start | bytes 1572868
  77.7 2.9 %copy-start.88 = (bf16[2,128,1,128]{3,2,1,0:T(2,128)(2,1)S(1)}, bf16[2,128,1,128]{3,2,1,0:T(2,128)(2,1)}, u32[]{:S(2)}) copy-start(bf16[2,128,1,128]{3,2,1,0:T(2,128)(2,1)} %get-tuple-element.38) | copy-start | bytes 196612
  79.3 3.3 %copy-start.87 = (bf16[2,128,1,128]{3,2,1,0:T(2,128)(2,1)S(1)}, bf16[2,128,1,128]{3,2,1,0:T(2,128)(2,1)}, u32[]{:S(2)}) copy-start(bf16[2,128,1,128]{3,2,1,0:T(2,128)(2,1)} %get-tuple-element.36) | copy-start | bytes 196612
  79.9 1.9 copy-start.78
  80.6 3.5 %copy-start.18 = (bf16[2,8,128,128]{3,2,1,0:T(8,128)(2,1)S(1)}, bf16[2,8,128,128]{3,2,1,0:T(8,128)(2,1)}, u32[]{:S(2)}) copy-start(bf16[2,8,128,128]{3,2,1,0:T(8,128)(2,1)} %get-tuple-element.46) | copy-start | bytes 1572868
  85.1 22.1 %all-to-all-start.2 = ((bf16[8,3,128,128]{3,2,1,0:T(8,128)(2,1)}), bf16[8,3,128,128]{3,2,1,0:T(8,128)(2,1)}, u32[]{:S(2)}, u32[]{:S(2)}) async-start(bf16[8,3,128,128]{3,2,1,0:T(8,128)(2,1)} %bitcast.23), calls=%async_computation.2 | async-start | bytes 1572864 | tf_op jit(solution)/shard_map/all_to_all | solution.py:100
  92.3 8.4 %copy-start.2 = (bf16[2,128,8,128]{1,3,2,0:T(8,128)(2,1)}, bf16[2,128,8,128]{1,3,2,0:T(8,128)(2,1)S(1)}, u32[]{:S(2)}) copy-start(bf16[2,128,8,128]{1,3,2,0:T(8,128)(2,1)S(1)} %fusion.61) | copy-start | bytes 1572868
  92.3 1.8 copy-start.21
  95.1 6.5 %copy-start.3 = (bf16[2,128,8,128]{1,3,2,0:T(8,128)(2,1)}, bf16[2,128,8,128]{1,3,2,0:T(8,128)(2,1)S(1)}, u32[]{:S(2)}) copy-start(bf16[2,128,8,128]{1,3,2,0:T(8,128)(2,1)S(1)} %fusion.62) | copy-start | bytes 1572868
  98.9 3.6 %copy-start.5 = (bf16[2,128,8,128]{1,3,2,0:T(8,128)(2,1)}, bf16[2,128,8,128]{1,3,2,0:T(8,128)(2,1)S(1)}, u32[]{:S(2)}) copy-start(bf16[2,128,8,128]{1,3,2,0:T(8,128)(2,1)S(1)} %fusion.63) | copy-start | bytes 1572868
  119.1 3.3 %copy-start.54 = (bf16[6,128,128]{1,2,0:T(8,128)(2,1)S(1)}, bf16[6,128,128]{1,2,0:T(8,128)(2,1)}, u32[]{:S(2)}) copy-start(bf16[6,128,128]{1,2,0:T(8,128)(2,1)} %copy.422) | copy-start | bytes 589828
  122.4 5.3 %copy-start.56 = (bf16[2,128,1,128]{1,3,0,2:T(8,128)(2,1)}, bf16[2,128,1,128]{1,3,0,2:T(8,128)(2,1)S(1)}, u32[]{:S(2)}) copy-start(bf16[2,128,1,128]{1,3,0,2:T(8,128)(2,1)S(1)} %fusion.54) | copy-start | bytes 196612
  122.8 4.9 %copy-start.58 = (bf16[2,128,1,128]{1,3,0,2:T(8,128)(2,1)}, bf16[2,128,1,128]{1,3,0,2:T(8,128)(2,1)S(1)}, u32[]{:S(2)}) copy-start(bf16[2,128,1,128]{1,3,0,2:T(8,128)(2,1)S(1)} %fusion.53) | copy-start | bytes 196612
  124.1 3.6 %copy-start.60 = (bf16[2,128,1,128]{1,3,0,2:T(8,128)(2,1)}, bf16[2,128,1,128]{1,3,0,2:T(8,128)(2,1)S(1)}, u32[]{:S(2)}) copy-start(bf16[2,128,1,128]{1,3,0,2:T(8,128)(2,1)S(1)} %fusion.52) | copy-start | bytes 196612
  130.7 13.8 %copy-start.42 = (f32[2,2,128,128]{3,2,1,0:T(8,128)}, f32[2,2,128,128]{3,2,1,0:T(8,128)S(1)}, u32[]{:S(2)}) copy-start(f32[2,2,128,128]{3,2,1,0:T(8,128)S(1)} %convolution_multiply_fusion.12) | copy-start | bytes 786436
  133.4 11.8 %copy-start.44 = (f32[2,2,128,128]{3,2,0,1:T(8,128)}, f32[2,2,128,128]{3,2,0,1:T(8,128)S(1)}, u32[]{:S(2)}) copy-start(f32[2,2,128,128]{3,2,0,1:T(8,128)S(1)} %convolution_multiply_fusion.13) | copy-start | bytes 786436
  136.1 9.8 %copy-start.46 = (f32[2,2,128,128]{3,2,0,1:T(8,128)}, f32[2,2,128,128]{3,2,0,1:T(8,128)S(1)}, u32[]{:S(2)}) copy-start(f32[2,2,128,128]{3,2,0,1:T(8,128)S(1)} %convolution_multiply_fusion.14) | copy-start | bytes 786436
  139.4 7.3 %copy-start.39 = (f32[2,2,128,128]{3,2,0,1:T(8,128)}, f32[2,2,128,128]{3,2,0,1:T(8,128)S(1)}, u32[]{:S(2)}) copy-start(f32[2,2,128,128]{3,2,0,1:T(8,128)S(1)} %convolution_multiply_fusion.15) | copy-start | bytes 786436
  152.2 22.8 %all-to-all-start.4 = ((bf16[8,3,128,128]{3,2,1,0:T(8,128)(2,1)}), bf16[8,3,128,128]{3,2,1,0:T(8,128)(2,1)S(1)}, u32[]{:S(2)}, u32[]{:S(2)}) async-start(bf16[8,3,128,128]{3,2,1,0:T(8,128)(2,1)} %get-tuple-element.75), calls=%async_computation.4 | async-start | bytes 1572864 | tf_op jit(solution)/shard_map/all_to_all | solution.py:224
  155.9 4.3 %copy-start.37 = (f32[2,2,128,128]{3,2,0,1:T(8,128)S(1)}, f32[2,2,128,128]{3,2,0,1:T(8,128)}, u32[]{:S(2)}) copy-start(f32[2,2,128,128]{3,2,0,1:T(8,128)} %fusion.94) | copy-start | bytes 786436
  156.7 3.5 %copy-start.68 = (f32[2,128,128]{2,1,0:T(8,128)S(1)}, f32[2,128,128]{2,1,0:T(8,128)}, u32[]{:S(2)}) copy-start(f32[2,128,128]{2,1,0:T(8,128)} %convert_element_type.251) | copy-start | bytes 393220
  156.7 36.0 %collective-permute-start.7 = (bf16[256,512]{1,0:T(8,128)(2,1)}, bf16[256,512]{1,0:T(8,128)(2,1)}, u32[]{:S(2)}, u32[]{:S(2)}) collective-permute-start(bf16[256,512]{1,0:T(8,128)(2,1)} %bitcast.644), channel_id=1, source_target_pairs={{0,8},{4,12},{8,0},{12,4},{16,24},{20,28},{24,16},{28,20},{1,9},{5... | collective-permute-start | bytes 786440 | tf_op jit(solution)/shard_map/ppermute | solution.py:12
  175.0 3.9 %copy-start.49 = (bf16[2,3,128,1,128]{4,2,1,0,3:T(8,128)(2,1)S(1)}, bf16[2,3,128,1,128]{4,2,1,0,3:T(8,128)(2,1)}, u32[]{:S(2)}) copy-start(bf16[2,3,128,1,128]{4,2,1,0,3:T(8,128)(2,1)} %fusion.33) | copy-start | bytes 589828
  175.0 3.9 %copy-start.50 = (bf16[2,3,128,1,128]{4,2,1,0,3:T(8,128)(2,1)S(1)}, bf16[2,3,128,1,128]{4,2,1,0,3:T(8,128)(2,1)}, u32[]{:S(2)}) copy-start(bf16[2,3,128,1,128]{4,2,1,0,3:T(8,128)(2,1)} %fusion.34) | copy-start | bytes 589828
  175.0 3.9 %copy-start.51 = (bf16[2,3,128,1,128]{4,2,1,0,3:T(8,128)(2,1)S(1)}, bf16[2,3,128,1,128]{4,2,1,0,3:T(8,128)(2,1)}, u32[]{:S(2)}) copy-start(bf16[2,3,128,1,128]{4,2,1,0,3:T(8,128)(2,1)} %fusion.35) | copy-start | bytes 589828
  175.0 4.0 %copy-start.52 = (bf16[2,3,128,1,128]{4,2,1,0,3:T(8,128)(2,1)S(1)}, bf16[2,3,128,1,128]{4,2,1,0,3:T(8,128)(2,1)}, u32[]{:S(2)}) copy-start(bf16[2,3,128,1,128]{4,2,1,0,3:T(8,128)(2,1)} %fusion.32) | copy-start | bytes 589828
  175.0 54.4 %all-to-all-start.3 = ((bf16[8,3,128,128]{3,2,1,0:T(8,128)(2,1)}), bf16[8,3,128,128]{3,2,1,0:T(8,128)(2,1)S(1)}, u32[]{:S(2)}, u32[]{:S(2)}) async-start(bf16[8,3,128,128]{3,2,1,0:T(8,128)(2,1)} %get-tuple-element.76), calls=%async_computation.3 | async-start | bytes 1572864 | tf_op jit(solution)/shard_map/all_to_all | solution.py:223
  185.6 6.4 %copy-start.40 = (f32[2,2,128,128]{3,2,0,1:T(8,128)S(1)}, f32[2,2,128,128]{3,2,0,1:T(8,128)}, u32[]{:S(2)}) copy-start(f32[2,2,128,128]{3,2,0,1:T(8,128)} %copy-done.39) | copy-start | bytes 786436
  185.7 31.5 %collective-permute-start.8 = (bf16[256,512]{1,0:T(8,128)(2,1)S(1)}, bf16[256,512]{1,0:T(8,128)(2,1)S(1)}, u32[]{:S(2)}, u32[]{:S(2)}) collective-permute-start(bf16[256,512]{1,0:T(8,128)(2,1)S(1)} %bitcast.675), channel_id=1, source_target_pairs={{0,16},{4,20},{8,24},{12,28},{16,0},{20,4},{24,8},{28,12},{1,17},{... | collective-permute-start | bytes 786440 | tf_op jit(solution)/shard_map/ppermute | solution.py:12
  188.5 28.9 %collective-permute-start.10 = (bf16[256,512]{1,0:T(8,128)(2,1)}, bf16[256,512]{1,0:T(8,128)(2,1)}, u32[]{:S(2)}, u32[]{:S(2)}) collective-permute-start(bf16[256,512]{1,0:T(8,128)(2,1)} %bitcast.640), channel_id=1, source_target_pairs={{0,8},{4,12},{8,0},{12,4},{16,24},{20,28},{24,16},{28,20},{1,9},{5... | collective-permute-start | bytes 786440 | tf_op jit(solution)/shard_map/ppermute | solution.py:12
  190.0 31.6 %collective-permute-start.11 = (bf16[256,512]{1,0:T(8,128)(2,1)}, bf16[256,512]{1,0:T(8,128)(2,1)}, u32[]{:S(2)}, u32[]{:S(2)}) collective-permute-start(bf16[256,512]{1,0:T(8,128)(2,1)} %bitcast.639), channel_id=1, source_target_pairs={{0,16},{4,20},{8,24},{12,28},{16,0},{20,4},{24,8},{28,12},{1,17},{... | collective-permute-start | bytes 786440 | tf_op jit(solution)/shard_map/ppermute | solution.py:12
  190.5 2.7 %copy-start.117 = (bf16[2,128,1,128]{3,1,0,2:T(8,128)(2,1)S(1)}, bf16[2,128,1,128]{3,1,0,2:T(8,128)(2,1)}, u32[]{:S(2)}) copy-start(bf16[2,128,1,128]{3,1,0,2:T(8,128)(2,1)} %fusion.59) | copy-start | bytes 196612
  190.5 2.7 %copy-start.118 = (bf16[2,128,1,128]{3,1,0,2:T(8,128)(2,1)S(1)}, bf16[2,128,1,128]{3,1,0,2:T(8,128)(2,1)}, u32[]{:S(2)}) copy-start(bf16[2,128,1,128]{3,1,0,2:T(8,128)(2,1)} %fusion.58) | copy-start | bytes 196612
  190.5 2.7 %copy-start.119 = (bf16[2,128,1,128]{3,1,0,2:T(8,128)(2,1)S(1)}, bf16[2,128,1,128]{3,1,0,2:T(8,128)(2,1)}, u32[]{:S(2)}) copy-start(bf16[2,128,1,128]{3,1,0,2:T(8,128)(2,1)} %fusion.57) | copy-start | bytes 196612
  190.5 33.0 %collective-permute-start.9 = (bf16[256,512]{1,0:T(8,128)(2,1)}, bf16[256,512]{1,0:T(8,128)(2,1)}, u32[]{:S(2)}, u32[]{:S(2)}) collective-permute-start(bf16[256,512]{1,0:T(8,128)(2,1)} %bitcast.641), channel_id=1, source_target_pairs={{0,4},{4,0},{8,12},{12,8},{16,20},{20,16},{24,28},{28,24},{1,5},{5... | collective-permute-start | bytes 786440 | tf_op jit(solution)/shard_map/ppermute | solution.py:12
  192.7 32.7 %collective-permute-start.6 = (bf16[256,512]{1,0:T(8,128)(2,1)}, bf16[256,512]{1,0:T(8,128)(2,1)}, u32[]{:S(2)}, u32[]{:S(2)}) collective-permute-start(bf16[256,512]{1,0:T(8,128)(2,1)} %bitcast.645), channel_id=1, source_target_pairs={{0,4},{4,0},{8,12},{12,8},{16,20},{20,16},{24,28},{28,24},{1,5},{5... | collective-permute-start | bytes 786440 | tf_op jit(solution)/shard_map/ppermute | solution.py:12
  (93 other events, 92.2 us)
where the time goes:
time: 237 us; the launch traced here: 234 us
  local copies, waits for them, and re-layouts  116 us (49%)
  starting transfers between devices  41.7 us (18%)
  waiting for transfers between devices  37 us (16%)
  matrix products  23.6 us (10%)
  other arithmetic  14.3 us (6%)
    unnamed x311, local copies, waits for them, and re-layouts  59.4 us
    ppermute x12, waiting for transfers between devices, swapped(): return lax.ppermute(value, axis, pairs)  23 us
    ppermute x12, starting transfers between devices, swapped(): return lax.ppermute(value, axis, pairs)  18.9 us
    dot_general x12, matrix products, slot_terms(): jnp.einsum('btks,btd->bksd', weights_low[:, :, first_slot:last_slot], gra...  10.6 us
    all_to_all x1, waiting for transfers between devices, local(): lax.all_to_all(send_values, 'seq', split_axis=0, concat_axis=0, tiled=True)  10.2 us
    slice x6, local copies, waits for them, and re-layouts, listed_rows(): rand_part[head_index]  9.83 us
    slice x6, local copies, waits for them, and re-layouts, listed_rows(): part_list = part_list + [far_arr[:, :, head_index] for far_arr in far_list]  6.99 us
    all_to_all x1, starting transfers between devices, local(): lax.all_to_all(key_pick.reshape(out_shape), 'seq', split_axis=0, concat_a...  6 us
  transfers between devices with their start and end apart: 17, of which 4 were waited for; matrix products, arithmetic and copies ran while one was open for 35% of the time, Pallas kernels for 0%

commit v1 on v0

v1 whole, which is shorter than its diff:
```python
import functools
import math

import jax
import jax.numpy as jnp
from jax import lax
from jax.experimental import pallas as pl
from jax.experimental.pallas import tpu as pltpu
from jax.sharding import PartitionSpec as P

KEYS, VALUES, QUERIES, GRADS, LISTS = range(5)


def flipped(index, mask):
    bit = 1
    while bit <= mask:
        if mask & bit:
            index = index + bit - 2 * bit * lax.rem(lax.div(index, bit), 2)
        bit *= 2
    return index


def kernel(
    dims,
    q_hbm, k_hbm, v_hbm, g_hbm, list_hbm,
    out_hbm, dq_hbm, dk_hbm, dv_hbm,
    qbuf, gbuf, kbuf, vbuf, ktbuf, vtbuf, obuf, dqbuf,
    dka, dva, segk, segv, redk, redv,
    list_vmem, list_smem, prev_smem, last_smem,
    in_send, in_recv, own_sem, relay_send, relay_recv,
    red_send, red_recv, ret_send, ret_recv, list_sem,
):
    groups, ranks, blks, rand, size, width = dims
    slot_count = ranks * groups * blks
    scale = 1.0 / math.sqrt(width)
    me = lax.axis_index("seq")
    group, rank = lax.div(me, ranks), lax.rem(me, ranks)
    f32, bf16 = jnp.float32, jnp.bfloat16

    def head_columns(head):
        return pl.ds(pl.multiple_of(head * width, width), width)

    def blocks(index):
        return pl.ds(index * blks, blks)

    def at_group(delta):
        return lax.rem(group + delta + groups, groups)

    def column_peer(other):
        return {"seq": other * ranks + rank}

    def row_peer(mask):
        return {"seq": group * ranks + flipped(rank, mask)}

    sources = (k_hbm, v_hbm, q_hbm, g_hbm)
    landing = (kbuf, vbuf, qbuf, gbuf)

    def scatter(which, delta):
        peer = at_group(delta)
        if which == LISTS:
            src, dst = list_hbm.at[peer], list_vmem.at[group]
        else:
            src = sources[which].at[:, :, head_columns(peer)]
            dst = landing[which].at[blocks(group)]
        if delta == 0:
            return pltpu.make_async_copy(src, dst, own_sem.at[which])
        return pltpu.make_async_remote_copy(
            src, dst, in_send.at[which, delta], in_recv.at[which, delta],
            device_id=column_peer(peer), device_id_type=pl.DeviceIdType.MESH,
        )

    def relay(which, delta, mask):
        source = at_group(-delta)
        if delta == 0:
            src = sources[which].at[:, :, head_columns(group)]
        else:
            src = landing[which].at[blocks(source)]
        return pltpu.make_async_remote_copy(
            src, landing[which].at[blocks(mask * groups + source)],
            relay_send.at[which, delta, mask], relay_recv.at[which, delta, mask],
            device_id=row_peer(mask), device_id_type=pl.DeviceIdType.MESH,
        )

    def reduce(which, step, mask):
        owner = at_group(step + 1)
        return pltpu.make_async_remote_copy(
            landing[which].at[blocks(mask * groups + owner)],
            (redk, redv)[which].at[blocks((mask - 1) * groups + owner)],
            red_send.at[which, step, mask], red_recv.at[which, step, mask],
            device_id=row_peer(mask), device_id_type=pl.DeviceIdType.MESH,
        )

    results = (dk_hbm, dv_hbm, out_hbm, dq_hbm)
    leaving = (kbuf, vbuf, obuf, dqbuf)

    def giveback(which, step, remote):
        owner = at_group(step + 1)
        src = leaving[which].at[blocks(owner)]
        dst = results[which].at[:, :, head_columns(group)]
        if not remote:
            return pltpu.make_async_copy(src, dst, ret_send.at[which, step])
        return pltpu.make_async_remote_copy(
            src, dst, ret_send.at[which, step], ret_recv.at[which, step],
            device_id=column_peer(owner), device_id_type=pl.DeviceIdType.MESH,
        )

    masks = range(1, ranks)
    deltas = range(1, groups)
    pair = (KEYS, VALUES)

    barrier = pltpu.get_barrier_semaphore()
    for delta in deltas:
        pl.semaphore_signal(
            barrier, inc=1, device_id=column_peer(at_group(delta)),
            device_id_type=pl.DeviceIdType.MESH,
        )
    for mask in masks:
        pl.semaphore_signal(
            barrier, inc=1, device_id=row_peer(mask), device_id_type=pl.DeviceIdType.MESH
        )
    pl.semaphore_wait(barrier, groups - 1 + ranks - 1)

    for delta in deltas:
        scatter(LISTS, delta).start()
    for delta in deltas:
        for which in pair:
            scatter(which, delta).start()
    for which in pair:
        for mask in masks:
            relay(which, 0, mask).start()
    for delta in deltas:
        for which in (QUERIES, GRADS):
            scatter(which, delta).start()
    for which in range(5):
        scatter(which, 0).start()

    scatter(LISTS, 0).wait()
    for delta in deltas:
        scatter(LISTS, delta).wait_recv()
    list_copy = pltpu.make_async_copy(list_vmem, list_smem, list_sem)
    list_copy.start()
    list_copy.wait()
    targets = []
    for step in range(groups):
        for lane in range(blks * rand):
            targets.append(list_smem[at_group(step + 1), 0, lane])
    for entry, target in enumerate(targets):
        found = jnp.int32(0)
        for earlier in range(entry):
            found = jnp.where(targets[earlier] == target, earlier + 1, found)
        prev_smem[entry] = found

    @pl.loop(0, slot_count)
    def _(slot):
        found = jnp.int32(0)
        for entry, target in enumerate(targets):
            found = jnp.where(target == slot, entry + 1, found)
        last_smem[slot] = found
        dka[slot] = jnp.zeros((size, width), f32)
        dva[slot] = jnp.zeros((size, width), f32)

    segk[0] = jnp.zeros((size, width), f32)
    segv[0] = jnp.zeros((size, width), f32)

    for delta in deltas:
        for which in pair:
            scatter(which, delta).wait_recv()
            for mask in masks:
                relay(which, delta, mask).start()
    for which in pair:
        scatter(which, 0).wait()

    def turn(low, high):
        @pl.loop(low, high)
        def _(slot):
            ktbuf[slot] = kbuf[slot].astype(f32).T.astype(bf16)
            vtbuf[slot] = vbuf[slot].astype(f32).T.astype(bf16)

    turn(0, groups * blks)
    for delta in range(groups):
        for which in pair:
            for mask in masks:
                relay(which, delta, mask).wait_recv()
    turn(groups * blks, slot_count)

    for which in (QUERIES, GRADS):
        scatter(which, 0).wait()
        for delta in deltas:
            scatter(which, delta).wait_recv()

    def dot(left, right, contract):
        return lax.dot_general(
            left, right, ((contract[:1], contract[1:]), ((), ())), preferred_element_type=f32
        )

    def rounded(value):
        return value.astype(bf16).astype(f32)

    def one_block(step, blk):
        owner = at_group(step + 1)
        here = owner * blks + blk
        query, grad = qbuf[here], gbuf[here]
        slots = [owner * blks + blk]
        bit = 1
        while bit < blks:
            slots.append(owner * blks + (blk ^ bit))
            bit *= 2
        bit = 1
        while bit < ranks:
            slots.append((bit * groups + owner) * blks + blk)
            bit *= 2
        bit = 1
        while bit < groups:
            slots.append(flipped(owner, bit) * blks + blk)
            bit *= 2
        fixed = len(slots)
        for pick in range(rand):
            slots.append(list_smem[owner, 0, blk * rand + pick])
        key_set = jnp.concatenate([kbuf[slot] for slot in slots], axis=0)
        value_set = jnp.concatenate([vbuf[slot] for slot in slots], axis=0)
        scores = dot(key_set, query, (1, 1)) * scale
        grad_weights = dot(value_set, grad, (1, 1))
        top = jnp.max(scores, axis=0, keepdims=True)
        raised = jnp.exp(scores - top)
        total = jnp.sum(raised, axis=0, keepdims=True)
        weights = raised * (1.0 / total)
        weights_low = weights.astype(bf16)
        value_turned = jnp.concatenate([vtbuf[slot] for slot in slots], axis=1)
        attn = rounded(dot(value_turned, weights_low, (1, 0)))
        obuf[here] = attn.T.astype(bf16)
        delta = jnp.sum(grad.astype(f32).T * attn, axis=0, keepdims=True)
        grad_scores = (weights * (grad_weights - delta)).astype(bf16)
        key_turned = jnp.concatenate([ktbuf[slot] for slot in slots], axis=1)
        dqbuf[here] = (dot(key_turned, grad_scores, (1, 0)) * scale).T.astype(bf16)
        key_terms = dot(grad_scores, query, (1, 0)) * scale
        value_terms = dot(weights_low, grad, (1, 0))
        for terms, total_ref, chain in ((key_terms, dka, segk), (value_terms, dva, segv)):
            for place, slot in enumerate(slots):
                term = terms[place * size : (place + 1) * size, :]
                if place:
                    term = rounded(term)
                if place < fixed:
                    total_ref[slot] += term
                else:
                    entry = (step * blks + blk) * rand + place - fixed
                    before = prev_smem[entry]
                    chain[entry + 1] = term + chain[before]

    @pl.loop(0, groups)
    def _(step):
        for blk in range(blks):
            one_block(step, blk)

        @pl.when(step < groups - 1)
        def _():
            for which in (2, 3):
                giveback(which, step, True).start()

        @pl.when(step == groups - 1)
        def _():
            for which in (2, 3):
                giveback(which, step, False).start()

    for delta in range(groups):
        for which in pair:
            for mask in masks:
                relay(which, delta, mask).wait_send()
    for step in range(groups):
        for which in pair:
            total_ref, chain = ((dka, segk), (dva, segv))[which]
            for mask in masks:
                first = (mask * groups + at_group(step + 1)) * blks
                for blk in range(blks):
                    here = first + blk
                    last = last_smem[here]
                    landing[which][here] = (
                        total_ref[here] + chain[last]
                    ).astype(bf16)
                reduce(which, step, mask).start()
    for step in range(groups):
        for which in pair:
            total_ref, chain = ((dka, segk), (dva, segv))[which]
            owner = at_group(step + 1)
            for mask in masks:
                reduce(which, step, mask).wait_recv()
            for blk in range(blks):
                here = owner * blks + blk
                last = last_smem[here]
                value = total_ref[here] + chain[last]
                for mask in masks:
                    there = ((mask - 1) * groups + owner) * blks + blk
                    value = value + (redk, redv)[which][there].astype(f32)
                landing[which][here] = value.astype(bf16)
            giveback(which, step, step < groups - 1).start()

    for delta in deltas:
        for which in range(5):
            scatter(which, delta).wait_send()
    for step in range(groups):
        for which in pair:
            for mask in masks:
                reduce(which, step, mask).wait_send()
        for which in (2, 3, 0, 1):
            if step < groups - 1:
                giveback(which, step, True).wait_send()
                giveback(which, step, True).wait_recv()
            else:
                giveback(which, step, False).wait()


def local(queries, keys, values, out_grad, rand_blocks):
    groups, blks, rand = rand_blocks.shape
    rows = queries.shape[0]
    size = rows // blks
    width = queries.shape[1] // groups
    ranks = lax.axis_size("seq") // groups
    slots = ranks * groups * blks
    entries = groups * blks * rand
    rank = lax.axis_index("seq") % ranks
    owner = rand_blocks // blks
    listed = (((owner % ranks) ^ rank) * groups + owner // ranks) * blks + rand_blocks % blks
    listed = listed.reshape(groups, 1, blks * rand)
    listed = jnp.pad(listed, ((0, 0), (0, 7), (0, 128 - blks * rand)))
    whole = jax.ShapeDtypeStruct((blks, size, groups * width), jnp.bfloat16)
    bf16, f32, dma = jnp.bfloat16, jnp.float32, pltpu.SemaphoreType.DMA
    flops = 12 * groups * blks * size * size * width * (rand + 1 + int(math.log2(slots)))
    arrays = [item.reshape(whole.shape) for item in (queries, keys, values, out_grad)]
    results = pl.pallas_call(
        functools.partial(kernel, (groups, ranks, blks, rand, size, width)),
        out_shape=[whole] * 4,
        in_specs=[pl.BlockSpec(memory_space=pl.ANY)] * 5,
        out_specs=[pl.BlockSpec(memory_space=pl.ANY)] * 4,
        scratch_shapes=[
            pltpu.VMEM((groups * blks, size, width), bf16),
            pltpu.VMEM((groups * blks, size, width), bf16),
            pltpu.VMEM((slots, size, width), bf16),
            pltpu.VMEM((slots, size, width), bf16),
            pltpu.VMEM((slots, width, size), bf16),
            pltpu.VMEM((slots, width, size), bf16),
            pltpu.VMEM((groups * blks, size, width), bf16),
            pltpu.VMEM((groups * blks, size, width), bf16),
            pltpu.VMEM((slots, size, width), f32),
            pltpu.VMEM((slots, size, width), f32),
            pltpu.VMEM((entries + 1, size, width), f32),
            pltpu.VMEM((entries + 1, size, width), f32),
            pltpu.VMEM(((ranks - 1) * groups * blks, size, width), bf16),
            pltpu.VMEM(((ranks - 1) * groups * blks, size, width), bf16),
            pltpu.VMEM((groups, 8, 128), jnp.int32),
            pltpu.SMEM((groups, 8, 128), jnp.int32),
            pltpu.SMEM((entries,), jnp.int32),
            pltpu.SMEM((slots,), jnp.int32),
            dma((5, groups)),
            dma((5, groups)),
            dma((5,)),
            dma((2, groups, ranks)),
            dma((2, groups, ranks)),
            dma((2, groups, ranks)),
            dma((2, groups, ranks)),
            dma((4, groups)),
            dma((4, groups)),
            dma,
        ],
        compiler_params=pltpu.CompilerParams(
            collective_id=0, has_side_effects=True, vmem_limit_bytes=56 * 2**20
        ),
        cost_estimate=pl.CostEstimate(
            flops=flops, bytes_accessed=16 * rows * groups * width, transcendentals=0
        ),
    )(*arrays, listed)
    return tuple(item.reshape(queries.shape) for item in results)


def solution(mesh):
    spec = P("seq", "head")
    return jax.shard_map(
        local,
        mesh=mesh,
        in_specs=(spec, spec, spec, spec, P("head", "seq", None)),
        out_specs=(spec, spec, spec, spec),
        check_vma=False,
    )
```

time: 237 us -> 61.4 us (0.26); the launches traced: 234 us -> 61.1 us
  local copies, waits for them, and re-layouts: 116 us -> 5.98 us
  Pallas kernels: 0 us -> 54.4 us
  starting transfers between devices: 41.7 us -> 0 us
  waiting for transfers between devices: 37 us -> 0 us
  matrix products: 23.6 us -> 0 us
  other arithmetic: 14.3 us -> 0.03 us
    pallas_call x0 -> x1, Pallas kernels: none -> 54.4 us  [local(): pl.pallas_call(functools.partial(kernel, (groups, ranks, blks, rand, size...]
    unnamed x311 -> x12, local copies, waits for them, and re-layouts: 59.4 us -> 5.18 us
    dot_general x42 -> x0, matrix products: 23.6 us -> none  [the longest x12 10.6 us: slot_terms(): jnp.einsum('btks,btd->bksd', weights_low[:, :, first_slot:last_slot], gra...]
    ppermute x12 -> x0, waiting for transfers between devices: 23 us -> none  [swapped(): return lax.ppermute(value, axis, pairs)]
    all_to_all x5 -> x0, starting transfers between devices: 22.8 us -> none  [the longest x1 6 us: local(): lax.all_to_all(key_pick.reshape(out_shape), 'seq', split_axis=0, concat_a...]
    slice x24 -> x0, local copies, waits for them, and re-layouts: 21.8 us -> none  [the longest x6 9.83 us: listed_rows(): rand_part[head_index]]
    ppermute x12 -> x0, starting transfers between devices: 18.9 us -> none  [swapped(): return lax.ppermute(value, axis, pairs)]
    all_to_all x5 -> x0, waiting for transfers between devices: 14.1 us -> none  [the longest x1 10.2 us: local(): lax.all_to_all(send_values, 'seq', split_axis=0, concat_axis=0, tiled=True)]
  transfers between devices with their start and end apart: 17 -> 0, of which waited for: 4 -> 0; matrix products, arithmetic and copies ran while one was open for 35% -> 0% of each run, Pallas kernels for 0% -> 0%
where the time goes in v1:
time: 61.4 us; the launch traced here: 61.1 us
  Pallas kernels  54.4 us (89%)
  local copies, waits for them, and re-layouts  5.98 us (10%)
  between operations  0.67 us (1%)
    pallas_call x1, Pallas kernels, local(): pl.pallas_call(functools.partial(kernel, (groups, ranks, blks, rand, size...  54.4 us
    unnamed x12, local copies, waits for them, and re-layouts  5.18 us

profile of v1, /device:TPU:0, one launch (start us, length us, event | category | flops | bytes accessed | tf_op | source)
XLA Modules:
  0.0 61.1 jit_solution(2060318718154482947)
XLA Ops:
  0.6 0.0 copy-start.3
  0.7 0.7 %copy-done.3 = s32[4,2,3]{0,1,2:T(2,128)S(1)} copy-done((s32[4,2,3]{0,1,2:T(2,128)S(1)}, s32[4,2,3]{0,1,2:T(2,128)}, u32[]{:S(2)}) %copy-start.3) | copy-done | bytes 120
  1.4 0.1 copy.11
  1.5 0.1 reshape.39
  1.5 0.6 %pad.4.list_hbm = s32[4,8,128]{2,1,0:T(8,128)} pad(s32[4,1,6]{2,1,0:T(1,128)S(1)} %bitcast.13, s32[]{:T(128)} %constant.48.clone.1), padding=0_0x0_7x0_122 | pad | bytes 16484 | tf_op jit(solution)/shard_map/jit(_pad)/pad | solution.py:323
  2.2 54.4 %shard_map.84 = (bf16[2,128,512]{2,1,0:T(8,128)(2,1)}, bf16[2,128,512]{2,1,0:T(8,128)(2,1)}, bf16[2,128,512]{2,1,0:T(8,128)(2,1)}, bf16[2,128,512]{2,1,0:T(8,128)(2,1)}) custom-call(bf16[2,128,512]{2,1,0:T(8,128)(2,1)} %bitcast.14, bf16[2,128,512]{2,1,0:T(8,128)(2,1)} %bitcast.15, bf16[2,128,512]{2,1,0:T(8,128)(2,1)} %bitcast.16, ...), custom_call_target="tpu_custom_call" | custom-call | flops 1610612736 | bytes 2097152 | tf_op jit(solution)/shard_map/pallas_call | solution.py:328
  56.6 0.0 copy-start.2
  56.6 1.7 %copy.17 = bf16[256,512]{1,0:T(8,128)(2,1)} copy(bf16[256,512]{1,0:T(8,128)(2,1)} %bitcast.12) | data formatting | bytes 524288
  58.3 0.0 copy-done.2
  58.3 0.0 copy-start.1
  58.3 0.7 %copy.18 = bf16[256,512]{1,0:T(8,128)(2,1)} copy(bf16[256,512]{1,0:T(8,128)(2,1)S(1)} %bitcast.11) | data formatting | bytes 524288
  59.0 0.3 copy-done.1
  59.4 0.0 copy-start
  59.4 0.7 %copy.19 = bf16[256,512]{1,0:T(8,128)(2,1)} copy(bf16[256,512]{1,0:T(8,128)(2,1)S(1)} %bitcast.10) | data formatting | bytes 524288
  60.1 0.3 copy-done
  60.4 0.7 %copy.20 = bf16[256,512]{1,0:T(8,128)(2,1)} copy(bf16[256,512]{1,0:T(8,128)(2,1)S(1)} %bitcast.9) | data formatting | bytes 524288
  (1 shorter events, 0.0 us)
Async XLA Ops:
  0.6 0.7 %copy-start.3 = (s32[4,2,3]{0,1,2:T(2,128)S(1)}, s32[4,2,3]{0,1,2:T(2,128)}, u32[]{:S(2)}) copy-start(s32[4,2,3]{0,1,2:T(2,128)} %param.9) | copy-start | bytes 292
  56.6 1.7 %copy-start.2 = (bf16[2,128,512]{2,1,0:T(8,128)(2,1)S(1)}, bf16[2,128,512]{2,1,0:T(8,128)(2,1)}, u32[]{:S(2)}) copy-start(bf16[2,128,512]{2,1,0:T(8,128)(2,1)} %get-tuple-element.9) | copy-start | bytes 786436
  58.3 1.0 %copy-start.1 = (bf16[2,128,512]{2,1,0:T(8,128)(2,1)S(1)}, bf16[2,128,512]{2,1,0:T(8,128)(2,1)}, u32[]{:S(2)}) copy-start(bf16[2,128,512]{2,1,0:T(8,128)(2,1)} %get-tuple-element.10) | copy-start | bytes 786436
  59.4 1.0 %copy-start = (bf16[2,128,512]{2,1,0:T(8,128)(2,1)S(1)}, bf16[2,128,512]{2,1,0:T(8,128)(2,1)}, u32[]{:S(2)}) copy-start(bf16[2,128,512]{2,1,0:T(8,128)(2,1)} %get-tuple-element.11) | copy-start | bytes 786436

commit v2 on v1

--- a/solution.py
+++ b/solution.py
@@ -44,7 +44,7 @@
         return pl.ds(index * blks, blks)
 
     def at_group(delta):
-        return lax.rem(group + delta + groups, groups)
+        return flipped(group, delta)
 
     def column_peer(other):
         return {"seq": other * ranks + rank}
@@ -70,7 +70,7 @@
         )
 
     def relay(which, delta, mask):
-        source = at_group(-delta)
+        source = at_group(delta)
         if delta == 0:
             src = sources[which].at[:, :, head_columns(group)]
         else:
@@ -82,7 +82,7 @@
         )
 
     def reduce(which, step, mask):
-        owner = at_group(step + 1)
+        owner = at_group(step)
         return pltpu.make_async_remote_copy(
             landing[which].at[blocks(mask * groups + owner)],
             (redk, redv)[which].at[blocks((mask - 1) * groups + owner)],
@@ -93,11 +93,11 @@
     results = (dk_hbm, dv_hbm, out_hbm, dq_hbm)
     leaving = (kbuf, vbuf, obuf, dqbuf)
 
-    def giveback(which, step, remote):
-        owner = at_group(step + 1)
+    def giveback(which, step):
+        owner = at_group(step)
         src = leaving[which].at[blocks(owner)]
         dst = results[which].at[:, :, head_columns(group)]
-        if not remote:
+        if step == 0:
             return pltpu.make_async_copy(src, dst, ret_send.at[which, step])
         return pltpu.make_async_remote_copy(
             src, dst, ret_send.at[which, step], ret_recv.at[which, step],
@@ -105,7 +105,7 @@
         )
 
     masks = range(1, ranks)
-    deltas = range(1, groups)
+    deltas = [*range(groups // 2, groups), *range(1, groups // 2)]
     pair = (KEYS, VALUES)
 
     barrier = pltpu.get_barrier_semaphore()
@@ -143,7 +143,7 @@
     targets = []
     for step in range(groups):
         for lane in range(blks * rand):
-            targets.append(list_smem[at_group(step + 1), 0, lane])
+            targets.append(list_smem[at_group(step), 0, lane])
     for entry, target in enumerate(targets):
         found = jnp.int32(0)
         for earlier in range(entry):
@@ -183,11 +183,6 @@
                 relay(which, delta, mask).wait_recv()
     turn(groups * blks, slot_count)
 
-    for which in (QUERIES, GRADS):
-        scatter(which, 0).wait()
-        for delta in deltas:
-            scatter(which, delta).wait_recv()
-
     def dot(left, right, contract):
         return lax.dot_general(
             left, right, ((contract[:1], contract[1:]), ((), ())), preferred_element_type=f32
@@ -196,8 +191,7 @@
     def rounded(value):
         return value.astype(bf16).astype(f32)
 
-    def one_block(step, blk):
-        owner = at_group(step + 1)
+    def one_block(step, owner, blk):
         here = owner * blks + blk
         query, grad = qbuf[here], gbuf[here]
         slots = [owner * blks + blk]
@@ -246,30 +240,26 @@
                     before = prev_smem[entry]
                     chain[entry + 1] = term + chain[before]
 
-    @pl.loop(0, groups)
-    def _(step):
+    for step in range(groups):
+        for which in (QUERIES, GRADS):
+            if step:
+                scatter(which, step).wait_recv()
+            else:
+                scatter(which, step).wait()
         for blk in range(blks):
-            one_block(step, blk)
-
-        @pl.when(step < groups - 1)
-        def _():
-            for which in (2, 3):
-                giveback(which, step, True).start()
-
-        @pl.when(step == groups - 1)
-        def _():
-            for which in (2, 3):
-                giveback(which, step, False).start()
+            one_block(step, at_group(step), blk)
+        for which in (2, 3):
+            giveback(which, step).start()
 
     for delta in range(groups):
         for which in pair:
             for mask in masks:
                 relay(which, delta, mask).wait_send()
-    for step in range(groups):
+    for step in (*deltas, 0):
         for which in pair:
             total_ref, chain = ((dka, segk), (dva, segv))[which]
             for mask in masks:
-                first = (mask * groups + at_group(step + 1)) * blks
+                first = (mask * groups + at_group(step)) * blks
                 for blk in range(blks):
                     here = first + blk
                     last = last_smem[here]
@@ -277,10 +267,10 @@
                         total_ref[here] + chain[last]
                     ).astype(bf16)
                 reduce(which, step, mask).start()
-    for step in range(groups):
+    for step in (*deltas, 0):
         for which in pair:
             total_ref, chain = ((dka, segk), (dva, segv))[which]
-            owner = at_group(step + 1)
+            owner = at_group(step)
             for mask in masks:
                 reduce(which, step, mask).wait_recv()
             for blk in range(blks):
@@ -291,21 +281,29 @@
                     there = ((mask - 1) * groups + owner) * blks + blk
                     value = value + (redk, redv)[which][there].astype(f32)
                 landing[which][here] = value.astype(bf16)
-            giveback(which, step, step < groups - 1).start()
+            giveback(which, step).start()
 
     for delta in deltas:
         for which in range(5):
             scatter(which, delta).wait_send()
-    for step in range(groups):
+    for step in (*deltas, 0):
         for which in pair:
             for mask in masks:
                 reduce(which, step, mask).wait_send()
         for which in (2, 3, 0, 1):
-            if step < groups - 1:
-                giveback(which, step, True).wait_send()
-                giveback(which, step, True).wait_recv()
-            else:
-                giveback(which, step, False).wait()
+            giveback(which, step).wait()
+
+
+def handed_out(*refs):
+    sources, targets, sem = refs[:4], refs[4:8], refs[8]
+    copies = [
+        pltpu.make_async_copy(source, target, sem.at[place])
+        for place, (source, target) in enumerate(zip(sources, targets))
+    ]
+    for copy in copies:
+        copy.start()
+    for copy in copies:
+        copy.wait()
 
 
 def local(queries, keys, values, out_grad, rand_blocks):
@@ -367,6 +365,16 @@
             flops=flops, bytes_accessed=16 * rows * groups * width, transcendentals=0
         ),
     )(*arrays, listed)
+    results = pl.pallas_call(
+        handed_out,
+        out_shape=[whole] * 4,
+        in_specs=[pl.BlockSpec(memory_space=pl.ANY)] * 4,
+        out_specs=[pl.BlockSpec(memory_space=pl.ANY)] * 4,
+        scratch_shapes=[dma((4,))],
+        cost_estimate=pl.CostEstimate(
+            flops=0, bytes_accessed=16 * rows * groups * width, transcendentals=0
+        ),
+    )(*results)
     return tuple(item.reshape(queries.shape) for item in results)
 
 

time: 61.4 us -> 90.7 us (1.48)
  Pallas kernels: 54.4 us -> 88.3 us
  local copies, waits for them, and re-layouts: 5.98 us -> 1.48 us
    pallas_call x0 -> x1, Pallas kernels: none -> 32.9 us  [local(): pl.pallas_call(handed_out, out_shape=[whole] * 4, in_specs=[pl.BlockSpec(...]
    unnamed x12 -> x2, local copies, waits for them, and re-layouts: 5.18 us -> 0.68 us
    pallas_call x1, Pallas kernels: 54.4 us -> 55.4 us  [local(): pl.pallas_call(functools.partial(kernel, (groups, ranks, blks, rand, size...]
where the time goes in v2:
time: 90.7 us; the launch traced here: 90.5 us
  Pallas kernels  88.3 us (97%)
  local copies, waits for them, and re-layouts  1.48 us (2%)
    pallas_call x1, Pallas kernels, local(): pl.pallas_call(functools.partial(kernel, (groups, ranks, blks, rand, size...  55.4 us
    pallas_call x1, Pallas kernels, local(): pl.pallas_call(handed_out, out_shape=[whole] * 4, in_specs=[pl.BlockSpec(...  32.9 us

profile of v2, /device:TPU:0, one launch (start us, length us, event | category | flops | bytes accessed | tf_op | source)
XLA Modules:
  0.0 90.5 jit_solution(3487484748268100427)
XLA Ops:
  0.6 0.0 copy-start
  0.7 0.7 copy-done
  1.4 0.1 copy.11
  1.5 0.1 reshape.39
  1.5 0.6 pad.4.list_hbm
  2.2 55.4 %shard_map.84 = (bf16[2,128,512]{2,1,0:T(8,128)(2,1)}, bf16[2,128,512]{2,1,0:T(8,128)(2,1)}, bf16[2,128,512]{2,1,0:T(8,128)(2,1)}, bf16[2,128,512]{2,1,0:T(8,128)(2,1)}) custom-call(bf16[2,128,512]{2,1,0:T(8,128)(2,1)} %bitcast.10, bf16[2,128,512]{2,1,0:T(8,128)(2,1)} %bitcast.11, bf16[2,128,512]{2,1,0:T(8,128)(2,1)} %bitcast.12, ...), custom_call_target="tpu_custom_call" | custom-call | flops 1610612736 | bytes 2097152 | tf_op jit(solution)/shard_map/pallas_call | solution.py:326
  57.6 32.9 %shard_map.85 = (bf16[2,128,512]{2,1,0:T(8,128)(2,1)}, bf16[2,128,512]{2,1,0:T(8,128)(2,1)}, bf16[2,128,512]{2,1,0:T(8,128)(2,1)}, bf16[2,128,512]{2,1,0:T(8,128)(2,1)}) custom-call(bf16[2,128,512]{2,1,0:T(8,128)(2,1)} %get-tuple-element.12.refs_0_, bf16[2,128,512]{2,1,0:T(8,128)(2,1)} %get-tuple-element.13.refs_1_, ...), custom_call_target="tpu_custom_call" | custom-call | bytes 2097152 | tf_op jit(solution)/shard_map/pallas_call | solution.py:368
  (1 shorter events, 0.0 us)
Async XLA Ops:
  0.6 0.7 copy-start

commit v3 on v1

--- a/solution.py
+++ b/solution.py
@@ -306,6 +306,11 @@
                 giveback(which, step, True).wait_recv()
             else:
                 giveback(which, step, False).wait()
+
+
+def handed_out(*refs):
+    for source, target in zip(refs[:4], refs[4:]):
+        target[...] = source[...]
 
 
 def local(queries, keys, values, out_grad, rand_blocks):
@@ -367,6 +372,13 @@
             flops=flops, bytes_accessed=16 * rows * groups * width, transcendentals=0
         ),
     )(*arrays, listed)
+    results = pl.pallas_call(
+        handed_out,
+        out_shape=[whole] * 4,
+        in_specs=[pl.BlockSpec(memory_space=pltpu.VMEM)] * 4,
+        out_specs=[pl.BlockSpec(memory_space=pltpu.VMEM)] * 4,
+        compiler_params=pltpu.CompilerParams(vmem_limit_bytes=16 * 2**20),
+    )(*results)
     return tuple(item.reshape(queries.shape) for item in results)
 
 

time: 61.4 us -> 61.7 us (level)
  Pallas kernels: 54.4 us -> 55.5 us
  local copies, waits for them, and re-layouts: 5.98 us -> 5.27 us
    pallas_call x0 -> x1, Pallas kernels: none -> 1.03 us  [local(): pl.pallas_call(handed_out, out_shape=[whole] * 4, in_specs=[pl.BlockSpec(...]
    unnamed x12 -> x10, local copies, waits for them, and re-layouts: 5.18 us -> 4.47 us
where the time goes in v3:
time: 61.7 us; the launch traced here: 61.4 us
  Pallas kernels  55.5 us (90%)
  local copies, waits for them, and re-layouts  5.27 us (9%)
  between operations  0.67 us (1%)
    pallas_call x1, Pallas kernels, local(): pl.pallas_call(functools.partial(kernel, (groups, ranks, blks, rand, size...  54.4 us
    unnamed x10, local copies, waits for them, and re-layouts  4.47 us

profile of v3, /device:TPU:0, one launch (start us, length us, event | category | flops | bytes accessed | tf_op | source)
XLA Modules:
  0.0 61.4 jit_solution(6263090085904323521)
XLA Ops:
  0.6 0.0 copy-start.4
  0.7 0.7 %copy-done.4 = s32[4,2,3]{0,1,2:T(2,128)S(1)} copy-done((s32[4,2,3]{0,1,2:T(2,128)S(1)}, s32[4,2,3]{0,1,2:T(2,128)}, u32[]{:S(2)}) %copy-start.4) | copy-done | bytes 120
  1.4 0.1 copy.11
  1.5 0.1 reshape.39
  1.5 0.6 pad.4.list_hbm
  2.2 54.4 %shard_map.84 = (bf16[2,128,512]{2,1,0:T(8,128)(2,1)}, bf16[2,128,512]{2,1,0:T(8,128)(2,1)}, bf16[2,128,512]{2,1,0:T(8,128)(2,1)}, bf16[2,128,512]{2,1,0:T(8,128)(2,1)}) custom-call(bf16[2,128,512]{2,1,0:T(8,128)(2,1)} %bitcast.10, bf16[2,128,512]{2,1,0:T(8,128)(2,1)} %bitcast.11, bf16[2,128,512]{2,1,0:T(8,128)(2,1)} %bitcast.12, ...), custom_call_target="tpu_custom_call" | custom-call | flops 1610612736 | bytes 2097152 | tf_op jit(solution)/shard_map/pallas_call | solution.py:333
  56.6 0.0 copy-start
  56.6 0.9 %copy-done = bf16[2,128,512]{2,1,0:T(8,128)(2,1)S(1)} copy-done((bf16[2,128,512]{2,1,0:T(8,128)(2,1)S(1)}, bf16[2,128,512]{2,1,0:T(8,128)(2,1)}, u32[]{:S(2)}) %copy-start) | copy-done | bytes 262168
  57.5 0.0 copy-start.1
  57.5 0.9 %copy-done.1 = bf16[2,128,512]{2,1,0:T(8,128)(2,1)S(1)} copy-done((bf16[2,128,512]{2,1,0:T(8,128)(2,1)S(1)}, bf16[2,128,512]{2,1,0:T(8,128)(2,1)}, u32[]{:S(2)}) %copy-start.1) | copy-done | bytes 262168
  58.5 0.0 copy-start.2
  58.5 0.9 %copy-done.2 = bf16[2,128,512]{2,1,0:T(8,128)(2,1)S(1)} copy-done((bf16[2,128,512]{2,1,0:T(8,128)(2,1)S(1)}, bf16[2,128,512]{2,1,0:T(8,128)(2,1)}, u32[]{:S(2)}) %copy-start.2) | copy-done | bytes 262168
  59.4 0.0 copy-start.3
  59.4 0.9 %copy-done.3 = bf16[2,128,512]{2,1,0:T(8,128)(2,1)S(1)} copy-done((bf16[2,128,512]{2,1,0:T(8,128)(2,1)S(1)}, bf16[2,128,512]{2,1,0:T(8,128)(2,1)}, u32[]{:S(2)}) %copy-start.3) | copy-done | bytes 262168
  60.4 1.0 %shard_map.85 = (bf16[2,128,512]{2,1,0:T(8,128)(2,1)}, bf16[2,128,512]{2,1,0:T(8,128)(2,1)}, bf16[2,128,512]{2,1,0:T(8,128)(2,1)}, bf16[2,128,512]{2,1,0:T(8,128)(2,1)}) custom-call(bf16[2,128,512]{2,1,0:T(8,128)(2,1)S(1)} %copy-done, bf16[2,128,512]{2,1,0:T(8,128)(2,1)S(1)} %copy-done.1, bf16[2,128,512]{2,1,0:T(8,128)(2,1)S(1)} %copy-done.2, ...), custom_call_target="tpu_custom_call" | custom-call | tf_op jit(solution)/shard_map/pallas_call | solution.py:375
  (1 shorter events, 0.0 us)
Async XLA Ops:
  0.6 0.7 %copy-start.4 = (s32[4,2,3]{0,1,2:T(2,128)S(1)}, s32[4,2,3]{0,1,2:T(2,128)}, u32[]{:S(2)}) copy-start(s32[4,2,3]{0,1,2:T(2,128)} %param.9) | copy-start | bytes 292
  56.6 1.0 %copy-start = (bf16[2,128,512]{2,1,0:T(8,128)(2,1)S(1)}, bf16[2,128,512]{2,1,0:T(8,128)(2,1)}, u32[]{:S(2)}) copy-start(bf16[2,128,512]{2,1,0:T(8,128)(2,1)} %get-tuple-element.12.refs_0_) | copy-start | bytes 786436
  57.5 0.9 %copy-start.1 = (bf16[2,128,512]{2,1,0:T(8,128)(2,1)S(1)}, bf16[2,128,512]{2,1,0:T(8,128)(2,1)}, u32[]{:S(2)}) copy-start(bf16[2,128,512]{2,1,0:T(8,128)(2,1)} %get-tuple-element.13.refs_1_) | copy-start | bytes 786436
  58.5 0.9 %copy-start.2 = (bf16[2,128,512]{2,1,0:T(8,128)(2,1)S(1)}, bf16[2,128,512]{2,1,0:T(8,128)(2,1)}, u32[]{:S(2)}) copy-start(bf16[2,128,512]{2,1,0:T(8,128)(2,1)} %get-tuple-element.14.refs_2_) | copy-start | bytes 786436
  59.4 0.9 %copy-start.3 = (bf16[2,128,512]{2,1,0:T(8,128)(2,1)S(1)}, bf16[2,128,512]{2,1,0:T(8,128)(2,1)}, u32[]{:S(2)}) copy-start(bf16[2,128,512]{2,1,0:T(8,128)(2,1)} %get-tuple-element.15.refs_3_) | copy-start | bytes 786436

commit v4 on v1

--- a/solution.py
+++ b/solution.py
@@ -62,7 +62,7 @@
         else:
             src = sources[which].at[:, :, head_columns(peer)]
             dst = landing[which].at[blocks(group)]
-        if delta == 0:
+        if isinstance(delta, int) and delta == 0:
             return pltpu.make_async_copy(src, dst, own_sem.at[which])
         return pltpu.make_async_remote_copy(
             src, dst, in_send.at[which, delta], in_recv.at[which, delta],
@@ -82,7 +82,7 @@
         )
 
     def reduce(which, step, mask):
-        owner = at_group(step + 1)
+        owner = at_group(-step)
         return pltpu.make_async_remote_copy(
             landing[which].at[blocks(mask * groups + owner)],
             (redk, redv)[which].at[blocks((mask - 1) * groups + owner)],
@@ -94,7 +94,7 @@
     leaving = (kbuf, vbuf, obuf, dqbuf)
 
     def giveback(which, step, remote):
-        owner = at_group(step + 1)
+        owner = at_group(-step)
         src = leaving[which].at[blocks(owner)]
         dst = results[which].at[:, :, head_columns(group)]
         if not remote:
@@ -128,9 +128,6 @@
     for which in pair:
         for mask in masks:
             relay(which, 0, mask).start()
-    for delta in deltas:
-        for which in (QUERIES, GRADS):
-            scatter(which, delta).start()
     for which in range(5):
         scatter(which, 0).start()
 
@@ -143,7 +140,7 @@
     targets = []
     for step in range(groups):
         for lane in range(blks * rand):
-            targets.append(list_smem[at_group(step + 1), 0, lane])
+            targets.append(list_smem[at_group(-step), 0, lane])
     for entry, target in enumerate(targets):
         found = jnp.int32(0)
         for earlier in range(entry):
@@ -167,6 +164,10 @@
             scatter(which, delta).wait_recv()
             for mask in masks:
                 relay(which, delta, mask).start()
+        for which in pair:
+            scatter(which, delta).wait_send()
+        for which in (QUERIES, GRADS):
+            scatter(which, delta).start()
     for which in pair:
         scatter(which, 0).wait()
 
@@ -185,8 +186,6 @@
 
     for which in (QUERIES, GRADS):
         scatter(which, 0).wait()
-        for delta in deltas:
-            scatter(which, delta).wait_recv()
 
     def dot(left, right, contract):
         return lax.dot_general(
@@ -197,7 +196,7 @@
         return value.astype(bf16).astype(f32)
 
     def one_block(step, blk):
-        owner = at_group(step + 1)
+        owner = at_group(-step)
         here = owner * blks + blk
         query, grad = qbuf[here], gbuf[here]
         slots = [owner * blks + blk]
@@ -248,15 +247,20 @@
 
     @pl.loop(0, groups)
     def _(step):
+        @pl.when(step > 0)
+        def _():
+            for which in (QUERIES, GRADS):
+                scatter(which, step).wait_recv()
+
         for blk in range(blks):
             one_block(step, blk)
 
-        @pl.when(step < groups - 1)
+        @pl.when(step > 0)
         def _():
             for which in (2, 3):
                 giveback(which, step, True).start()
 
-        @pl.when(step == groups - 1)
+        @pl.when(step == 0)
         def _():
             for which in (2, 3):
                 giveback(which, step, False).start()
@@ -265,11 +269,11 @@
         for which in pair:
             for mask in masks:
                 relay(which, delta, mask).wait_send()
-    for step in range(groups):
+    for step in (*deltas, 0):
         for which in pair:
             total_ref, chain = ((dka, segk), (dva, segv))[which]
             for mask in masks:
-                first = (mask * groups + at_group(step + 1)) * blks
+                first = (mask * groups + at_group(-step)) * blks
                 for blk in range(blks):
                     here = first + blk
                     last = last_smem[here]
@@ -277,10 +281,10 @@
                         total_ref[here] + chain[last]
                     ).astype(bf16)
                 reduce(which, step, mask).start()
-    for step in range(groups):
+    for step in (*deltas, 0):
         for which in pair:
             total_ref, chain = ((dka, segk), (dva, segv))[which]
-            owner = at_group(step + 1)
+            owner = at_group(-step)
             for mask in masks:
                 reduce(which, step, mask).wait_recv()
             for blk in range(blks):
@@ -291,17 +295,17 @@
                     there = ((mask - 1) * groups + owner) * blks + blk
                     value = value + (redk, redv)[which][there].astype(f32)
                 landing[which][here] = value.astype(bf16)
-            giveback(which, step, step < groups - 1).start()
-
-    for delta in deltas:
-        for which in range(5):
+            giveback(which, step, step > 0).start()
+
+    for delta in deltas:
+        for which in (LISTS, QUERIES, GRADS):
             scatter(which, delta).wait_send()
-    for step in range(groups):
+    for step in (*deltas, 0):
         for which in pair:
             for mask in masks:
                 reduce(which, step, mask).wait_send()
         for which in (2, 3, 0, 1):
-            if step < groups - 1:
+            if step > 0:
                 giveback(which, step, True).wait_send()
                 giveback(which, step, True).wait_recv()
             else:

time: 61.4 us -> 61.2 us (level)
  no operation moved by 1% of the time
where the time goes in v4:
time: 61.2 us; the launch traced here: 60.9 us
  Pallas kernels  54.2 us (89%)
  local copies, waits for them, and re-layouts  5.98 us (10%)
  between operations  0.67 us (1%)
    pallas_call x1, Pallas kernels, local(): pl.pallas_call(functools.partial(kernel, (groups, ranks, blks, rand, size...  54.2 us
    unnamed x12, local copies, waits for them, and re-layouts  5.18 us

profile of v4, /device:TPU:0, one launch (start us, length us, event | category | flops | bytes accessed | tf_op | source)
XLA Modules:
  0.0 60.9 jit_solution(9647013521213700468)
XLA Ops:
  0.6 0.0 copy-start.3
  0.7 0.7 %copy-done.3 = s32[4,2,3]{0,1,2:T(2,128)S(1)} copy-done((s32[4,2,3]{0,1,2:T(2,128)S(1)}, s32[4,2,3]{0,1,2:T(2,128)}, u32[]{:S(2)}) %copy-start.3) | copy-done | bytes 120
  1.4 0.1 copy.11
  1.5 0.1 reshape.39
  1.5 0.6 %pad.4.list_hbm = s32[4,8,128]{2,1,0:T(8,128)} pad(s32[4,1,6]{2,1,0:T(1,128)S(1)} %bitcast.13, s32[]{:T(128)} %constant.48.clone.1), padding=0_0x0_7x0_122 | pad | bytes 16484 | tf_op jit(solution)/shard_map/jit(_pad)/pad | solution.py:327
  2.2 54.2 %shard_map.84 = (bf16[2,128,512]{2,1,0:T(8,128)(2,1)}, bf16[2,128,512]{2,1,0:T(8,128)(2,1)}, bf16[2,128,512]{2,1,0:T(8,128)(2,1)}, bf16[2,128,512]{2,1,0:T(8,128)(2,1)}) custom-call(bf16[2,128,512]{2,1,0:T(8,128)(2,1)} %bitcast.14, bf16[2,128,512]{2,1,0:T(8,128)(2,1)} %bitcast.15, bf16[2,128,512]{2,1,0:T(8,128)(2,1)} %bitcast.16, ...), custom_call_target="tpu_custom_call" | custom-call | flops 1610612736 | bytes 2097152 | tf_op jit(solution)/shard_map/pallas_call | solution.py:332
  56.4 0.0 copy-start.2
  56.4 1.7 %copy.17 = bf16[256,512]{1,0:T(8,128)(2,1)} copy(bf16[256,512]{1,0:T(8,128)(2,1)} %bitcast.12) | data formatting | bytes 524288
  58.1 0.0 copy-done.2
  58.1 0.0 copy-start.1
  58.1 0.7 %copy.18 = bf16[256,512]{1,0:T(8,128)(2,1)} copy(bf16[256,512]{1,0:T(8,128)(2,1)S(1)} %bitcast.11) | data formatting | bytes 524288
  58.8 0.3 copy-done.1
  59.2 0.0 copy-start
  59.2 0.7 %copy.19 = bf16[256,512]{1,0:T(8,128)(2,1)} copy(bf16[256,512]{1,0:T(8,128)(2,1)S(1)} %bitcast.10) | data formatting | bytes 524288
  59.9 0.3 copy-done
  60.2 0.7 %copy.20 = bf16[256,512]{1,0:T(8,128)(2,1)} copy(bf16[256,512]{1,0:T(8,128)(2,1)S(1)} %bitcast.9) | data formatting | bytes 524288
  (1 shorter events, 0.0 us)
Async XLA Ops:
  0.6 0.7 %copy-start.3 = (s32[4,2,3]{0,1,2:T(2,128)S(1)}, s32[4,2,3]{0,1,2:T(2,128)}, u32[]{:S(2)}) copy-start(s32[4,2,3]{0,1,2:T(2,128)} %param.9) | copy-start | bytes 292
  56.4 1.7 %copy-start.2 = (bf16[2,128,512]{2,1,0:T(8,128)(2,1)S(1)}, bf16[2,128,512]{2,1,0:T(8,128)(2,1)}, u32[]{:S(2)}) copy-start(bf16[2,128,512]{2,1,0:T(8,128)(2,1)} %get-tuple-element.9) | copy-start | bytes 786436
  58.1 1.0 %copy-start.1 = (bf16[2,128,512]{2,1,0:T(8,128)(2,1)S(1)}, bf16[2,128,512]{2,1,0:T(8,128)(2,1)}, u32[]{:S(2)}) copy-start(bf16[2,128,512]{2,1,0:T(8,128)(2,1)} %get-tuple-element.10) | copy-start | bytes 786436
  59.2 1.0 %copy-start = (bf16[2,128,512]{2,1,0:T(8,128)(2,1)S(1)}, bf16[2,128,512]{2,1,0:T(8,128)(2,1)}, u32[]{:S(2)}) copy-start(bf16[2,128,512]{2,1,0:T(8,128)(2,1)} %get-tuple-element.11) | copy-start | bytes 786436

commit v5 on v4

--- a/solution.py
+++ b/solution.py
@@ -105,7 +105,7 @@
         )
 
     masks = range(1, ranks)
-    deltas = range(1, groups)
+    deltas = [(turn % 2) * (groups // 2) + turn // 2 for turn in range(1, groups)]
     pair = (KEYS, VALUES)
 
     barrier = pltpu.get_barrier_semaphore()
@@ -138,7 +138,7 @@
     list_copy.start()
     list_copy.wait()
     targets = []
-    for step in range(groups):
+    for step in (0, *deltas):
         for lane in range(blks * rand):
             targets.append(list_smem[at_group(-step), 0, lane])
     for entry, target in enumerate(targets):
@@ -195,7 +195,7 @@
     def rounded(value):
         return value.astype(bf16).astype(f32)
 
-    def one_block(step, blk):
+    def one_block(order, step, blk):
         owner = at_group(-step)
         here = owner * blks + blk
         query, grad = qbuf[here], gbuf[here]
@@ -241,19 +241,21 @@
                 if place < fixed:
                     total_ref[slot] += term
                 else:
-                    entry = (step * blks + blk) * rand + place - fixed
+                    entry = (order * blks + blk) * rand + place - fixed
                     before = prev_smem[entry]
                     chain[entry + 1] = term + chain[before]
 
     @pl.loop(0, groups)
-    def _(step):
+    def _(order):
+        step = lax.rem(order, 2) * (groups // 2) + lax.div(order, 2)
+
         @pl.when(step > 0)
         def _():
             for which in (QUERIES, GRADS):
                 scatter(which, step).wait_recv()
 
         for blk in range(blks):
-            one_block(step, blk)
+            one_block(order, step, blk)
 
         @pl.when(step > 0)
         def _():

time: 61.2 us -> 59.1 us (0.966)
  Pallas kernels: 54.2 us -> 52.2 us
    pallas_call x1, Pallas kernels: 54.2 us -> 52.2 us  [local(): pl.pallas_call(functools.partial(kernel, (groups, ranks, blks, rand, size...]
where the time goes in v5:
time: 59.1 us; the launch traced here: 58.9 us
  Pallas kernels  52.2 us (88%)
  local copies, waits for them, and re-layouts  5.98 us (10%)
  between operations  0.67 us (1%)
    pallas_call x1, Pallas kernels, local(): pl.pallas_call(functools.partial(kernel, (groups, ranks, blks, rand, size...  52.2 us
    unnamed x12, local copies, waits for them, and re-layouts  5.18 us

profile of v5, /device:TPU:0, one launch (start us, length us, event | category | flops | bytes accessed | tf_op | source)
XLA Modules:
  0.0 58.9 jit_solution(13937988551946821431)
XLA Ops:
  0.6 0.0 copy-start.3
  0.7 0.7 %copy-done.3 = s32[4,2,3]{0,1,2:T(2,128)S(1)} copy-done((s32[4,2,3]{0,1,2:T(2,128)S(1)}, s32[4,2,3]{0,1,2:T(2,128)}, u32[]{:S(2)}) %copy-start.3) | copy-done | bytes 120
  1.4 0.1 copy.11
  1.5 0.1 reshape.39
  1.5 0.6 %pad.4.list_hbm = s32[4,8,128]{2,1,0:T(8,128)} pad(s32[4,1,6]{2,1,0:T(1,128)S(1)} %bitcast.13, s32[]{:T(128)} %constant.48.clone.1), padding=0_0x0_7x0_122 | pad | bytes 16484 | tf_op jit(solution)/shard_map/jit(_pad)/pad | solution.py:329
  2.2 52.2 %shard_map.84 = (bf16[2,128,512]{2,1,0:T(8,128)(2,1)}, bf16[2,128,512]{2,1,0:T(8,128)(2,1)}, bf16[2,128,512]{2,1,0:T(8,128)(2,1)}, bf16[2,128,512]{2,1,0:T(8,128)(2,1)}) custom-call(bf16[2,128,512]{2,1,0:T(8,128)(2,1)} %bitcast.14, bf16[2,128,512]{2,1,0:T(8,128)(2,1)} %bitcast.15, bf16[2,128,512]{2,1,0:T(8,128)(2,1)} %bitcast.16, ...), custom_call_target="tpu_custom_call" | custom-call | flops 1610612736 | bytes 2097152 | tf_op jit(solution)/shard_map/pallas_call | solution.py:334
  54.4 0.0 copy-start.2
  54.4 1.7 %copy.17 = bf16[256,512]{1,0:T(8,128)(2,1)} copy(bf16[256,512]{1,0:T(8,128)(2,1)} %bitcast.12) | data formatting | bytes 524288
  56.1 0.0 copy-done.2
  56.1 0.0 copy-start.1
  56.1 0.7 %copy.18 = bf16[256,512]{1,0:T(8,128)(2,1)} copy(bf16[256,512]{1,0:T(8,128)(2,1)S(1)} %bitcast.11) | data formatting | bytes 524288
  56.8 0.3 copy-done.1
  57.1 0.0 copy-start
  57.1 0.7 %copy.19 = bf16[256,512]{1,0:T(8,128)(2,1)} copy(bf16[256,512]{1,0:T(8,128)(2,1)S(1)} %bitcast.10) | data formatting | bytes 524288
  57.8 0.3 copy-done
  58.2 0.7 %copy.20 = bf16[256,512]{1,0:T(8,128)(2,1)} copy(bf16[256,512]{1,0:T(8,128)(2,1)S(1)} %bitcast.9) | data formatting | bytes 524288
  (1 shorter events, 0.0 us)
Async XLA Ops:
  0.6 0.7 %copy-start.3 = (s32[4,2,3]{0,1,2:T(2,128)S(1)}, s32[4,2,3]{0,1,2:T(2,128)}, u32[]{:S(2)}) copy-start(s32[4,2,3]{0,1,2:T(2,128)} %param.9) | copy-start | bytes 292
  54.4 1.7 %copy-start.2 = (bf16[2,128,512]{2,1,0:T(8,128)(2,1)S(1)}, bf16[2,128,512]{2,1,0:T(8,128)(2,1)}, u32[]{:S(2)}) copy-start(bf16[2,128,512]{2,1,0:T(8,128)(2,1)} %get-tuple-element.9) | copy-start | bytes 786436
  56.1 1.0 %copy-start.1 = (bf16[2,128,512]{2,1,0:T(8,128)(2,1)S(1)}, bf16[2,128,512]{2,1,0:T(8,128)(2,1)}, u32[]{:S(2)}) copy-start(bf16[2,128,512]{2,1,0:T(8,128)(2,1)} %get-tuple-element.10) | copy-start | bytes 786436
  57.1 1.0 %copy-start = (bf16[2,128,512]{2,1,0:T(8,128)(2,1)S(1)}, bf16[2,128,512]{2,1,0:T(8,128)(2,1)}, u32[]{:S(2)}) copy-start(bf16[2,128,512]{2,1,0:T(8,128)(2,1)} %get-tuple-element.11) | copy-start | bytes 786436
